TPU v7x, 32 devices: a whole 2x2x4 slice. The times are simulated.
32 devices in a mesh: seq: 8 (over z, core), head: 4 (over y, x).
Axes of the slice: x: 2, y: 2, z: 4, core: 2. Of those that a mesh axis runs over, the one named last changes fastest.
Arguments:
- queries: bfloat16 [3072, 16384], P('seq', 'head'), may hold values from -5 to 5
- keys: bfloat16 [3072, 1024], P('seq', 'head'), may hold values from -5 to 5
- values: bfloat16 [3072, 1024], P('seq', 'head'), may hold values from -6 to 6
- feat_q: bfloat16 [128, 128, 128], P('head'), may hold values from -0.5 to 0.5
- feat_k: bfloat16 [128, 128, 128], P('head'), may hold values from -0.5 to 0.5
Outputs:
- grad_feat_q: float32 [128, 128, 128], P('head')
- grad_feat_k: float32 [128, 128, 128], P('head')
All inputs are finite; a program needn't handle non-finite values.
Results may differ from a plain program's by a relative error of at most 0.02.
Values may be sent and summed in bfloat16 or wider, within the bound.
No kernel may reach another device: no remote copies, remote signals or barrier semaphores. Data moves between devices by JAX's collectives and lax.ppermute only.
A program may use at most 128 MiB of HBM per device.

v0:
```python
import math

import jax
import jax.numpy as jnp
from jax import lax
from jax.sharding import PartitionSpec as P

HEADS = 128
KV_HEADS = 8


HIGHEST_MODE = lax.Precision.HIGHEST
MASKED_SCORE = -1e30


def from_partner(block, axis, stride):
    count = lax.axis_size(axis)
    route = []
    for low in range(count):
        high = low | 1 << stride
        if high != low and high < count:
            route += [(low, high), (high, low)]
    return lax.ppermute(block, axis, route)


def split_wide(entries):
    high = entries.astype(jnp.bfloat16)
    low = (entries - high.astype(jnp.float32)).astype(jnp.bfloat16)
    return (high, low)


def wide_left(form, wide, narrow):
    high, low = split_wide(wide)
    return jnp.einsum(form, high, narrow, preferred_element_type=jnp.float32) + jnp.einsum(
        form, low, narrow, preferred_element_type=jnp.float32
    )


def wide_right(form, narrow, wide):
    high, low = split_wide(wide)
    return jnp.einsum(form, narrow, high, preferred_element_type=jnp.float32) + jnp.einsum(
        form, narrow, low, preferred_element_type=jnp.float32
    )


def attend_block(
    running, query_half, query_pos, key_rows, value_rows, key_first, group_count, score_scale
):
    row_peak, row_total, summed = running
    half_rows = query_half.shape[0]
    key_count = key_rows.shape[0]
    head_dim = key_rows.shape[1] // group_count
    grouped = query_half.reshape(half_rows, group_count, -1, head_dim)
    key_heads = key_rows.reshape(key_count, group_count, head_dim)
    value_heads = value_rows.reshape(key_count, group_count, head_dim)
    scores = (
        jnp.einsum("rgjd,kgd->gjrk", grouped, key_heads, preferred_element_type=jnp.float32)
        * score_scale
    )
    scores = scores.reshape(row_peak.shape[0], half_rows, key_count)
    key_pos = key_first + jnp.arange(key_count, dtype=jnp.int32)
    allowed = (key_pos[None, :] <= query_pos[:, None])[None]
    new_peak = jnp.maximum(row_peak, jnp.max(jnp.where(allowed, scores, MASKED_SCORE), axis=-1))
    weights = jnp.exp(jnp.where(allowed, scores - new_peak[..., None], MASKED_SCORE))
    factor = jnp.exp(row_peak - new_peak)
    row_total = row_total * factor + jnp.sum(weights, axis=-1)
    rounded = weights.astype(jnp.bfloat16).reshape(group_count, -1, half_rows, key_count)
    mixture = jnp.einsum("gjrk,kgd->gjrd", rounded, value_heads, preferred_element_type=jnp.float32)
    summed = summed * factor[..., None] + mixture.reshape(summed.shape)
    return (new_peak, row_total, summed)


def body(queries, keys, values, feat_q, feat_k):
    row_count = queries.shape[0]
    heads_here = feat_q.shape[0]
    head_dim = feat_q.shape[1]
    seq_count = lax.axis_size("seq")
    seq_place = lax.axis_index("seq")
    head_place = lax.axis_index("head")
    spread = max(1, HEADS // KV_HEADS // heads_here)
    key_value = jnp.stack((keys, values))
    for bit_index in range(spread.bit_length() - 1):
        partner = from_partner(key_value, "head", bit_index)
        upper_half = head_place // (1 << bit_index) % 2 == 1
        key_value = jnp.where(
            upper_half,
            jnp.concatenate((partner, key_value), axis=2),
            jnp.concatenate((key_value, partner), axis=2),
        )
    group_count = key_value.shape[2] // head_dim
    group_size = heads_here // group_count
    query_pos = seq_place * row_count + jnp.arange(row_count, dtype=jnp.int32)
    half_rows = row_count // 2
    query_halves = (queries[:half_rows], queries[half_rows:])
    pos_halves = (query_pos[:half_rows], query_pos[half_rows:])
    top_halves = (jnp.max(pos_halves[0]), jnp.max(pos_halves[1]))
    score_scale = head_dim ** (-0.5)
    start_half = (
        jnp.full((heads_here, half_rows), MASKED_SCORE, jnp.float32),
        jnp.zeros((heads_here, half_rows), jnp.float32),
        jnp.zeros((heads_here, half_rows, head_dim), jnp.float32),
    )
    shard_part = lax.all_gather(key_value, "seq", axis=1, tiled=True)
    part_rows = shard_part.shape[1]
    block_rows = math.gcd(part_rows, 512)

    def one_step(step_index, halves_state):
        offset = step_index * block_rows
        key_rows = lax.dynamic_slice_in_dim(shard_part[0], offset, block_rows, 0)
        value_rows = lax.dynamic_slice_in_dim(shard_part[1], offset, block_rows, 0)
        updated = []
        for half_index in range(2):

            def attend_half(current, half_index=half_index):
                return attend_block(
                    current,
                    query_halves[half_index],
                    pos_halves[half_index],
                    key_rows,
                    value_rows,
                    offset,
                    group_count,
                    score_scale,
                )

            def unchanged(current):
                return current

            updated.append(
                lax.cond(
                    top_halves[half_index] >= offset,
                    attend_half,
                    unchanged,
                    halves_state[half_index],
                )
            )
        return tuple(updated)

    finished = lax.fori_loop(0, part_rows // block_rows, one_step, (start_half, start_half))
    teacher_out = jnp.concatenate(
        [
            (finished[half_index][2] / finished[half_index][1][..., None]).astype(jnp.bfloat16)
            for half_index in range(2)
        ],
        axis=1,
    )
    key_local = key_value[0].reshape(row_count, group_count, head_dim)
    value_local = key_value[1].reshape(row_count, group_count, head_dim)
    query_local = queries.reshape(row_count, heads_here, head_dim)
    query_pre = jnp.einsum("rhd,hdf->hrf", query_local, feat_q, preferred_element_type=jnp.float32)
    key_pre = jnp.einsum(
        "rgd,gjdf->gjrf",
        key_local,
        feat_k.reshape(group_count, group_size, head_dim, -1),
        preferred_element_type=jnp.float32,
    ).reshape(heads_here, row_count, -1)
    feat_count = query_pre.shape[-1]
    query_feat = jax.nn.softplus(query_pre).astype(jnp.bfloat16)
    key_feat = jax.nn.softplus(key_pre).astype(jnp.bfloat16)
    block_state = jnp.einsum(
        "gjrf,rgd->gjfd",
        key_feat.reshape(group_count, group_size, row_count, -1),
        value_local,
        preferred_element_type=jnp.float32,
    ).reshape(heads_here, feat_count, head_dim)
    block_norm = jnp.sum(key_feat, axis=1, dtype=jnp.float32)
    zero_pair = (jnp.zeros_like(block_state), jnp.zeros_like(block_norm))
    take_shard_part = (
        lax.all_gather(block_state[None].astype(jnp.bfloat16), "seq", axis=0, tiled=True).astype(
            jnp.float32
        ),
        lax.all_gather(block_norm[None].astype(jnp.bfloat16), "seq", axis=0, tiled=True).astype(
            jnp.float32
        ),
    )
    part_count = take_shard_part[0].shape[0]
    chosen = jnp.arange(part_count, dtype=jnp.int32) < seq_place
    before_state = zero_pair[0] + jnp.sum(
        jnp.where(chosen[:, None, None, None], take_shard_part[0], 0.0), axis=0
    )
    before_norm = zero_pair[1] + jnp.sum(
        jnp.where(chosen[:, None, None], take_shard_part[1], 0.0), axis=0
    )
    causal = jnp.arange(row_count)[:, None] >= jnp.arange(row_count)[None, :]
    affinity = jnp.einsum("hrf,hsf->hrs", query_feat, key_feat, preferred_element_type=jnp.float32)
    masked = jnp.where(causal[None], affinity, 0.0)
    local_mix = jnp.einsum(
        "gjrs,sgd->gjrd",
        masked.astype(jnp.bfloat16).reshape(group_count, group_size, row_count, row_count),
        value_local,
        preferred_element_type=jnp.float32,
    ).reshape(heads_here, row_count, head_dim)
    numerator = wide_right("hrf,hfd->hrd", query_feat, before_state) + local_mix
    denominator = wide_right("hrf,hf->hr", query_feat, before_norm) + jnp.sum(masked, axis=-1)
    student = numerator / denominator[..., None]
    total_tokens = row_count * seq_count
    grad_out = 2.0 * (student - teacher_out.astype(jnp.float32)) / total_tokens
    grad_numer = grad_out / denominator[..., None]
    grad_denom = -jnp.sum(grad_out * student, axis=-1) / denominator
    back_state = wide_right("hrf,hrd->hfd", query_feat, grad_numer)
    back_norm = wide_right("hrf,hr->hf", query_feat, grad_denom)

    def take_upper(running, shard_part):
        part_count = shard_part[0].shape[0]
        chosen = jnp.arange(part_count, dtype=jnp.int32) > seq_place
        return (
            running[0]
            + jnp.sum(jnp.where(chosen[:, None, None, None], shard_part[0], 0.0), axis=0),
            running[1] + jnp.sum(jnp.where(chosen[:, None, None], shard_part[1], 0.0), axis=0),
        )

    after_state, after_norm = take_upper(
        zero_pair,
        (
            lax.all_gather(back_state[None].astype(jnp.bfloat16), "seq", axis=0, tiled=True).astype(
                jnp.float32
            ),
            lax.all_gather(back_norm[None].astype(jnp.bfloat16), "seq", axis=0, tiled=True).astype(
                jnp.float32
            ),
        ),
    )
    grad_aff = wide_left(
        "gjrd,sgd->gjrs",
        grad_numer.reshape(group_count, group_size, row_count, head_dim),
        value_local,
    ).reshape(heads_here, row_count, row_count)
    grad_aff = jnp.where(causal[None], grad_aff + grad_denom[..., None], 0.0)
    grad_qfeat = (
        jnp.einsum("hrd,hfd->hrf", grad_numer, before_state, precision=HIGHEST_MODE)
        + grad_denom[..., None] * before_norm[:, None, :]
        + wide_left("hrs,hsf->hrf", grad_aff, key_feat)
    )
    grad_kfeat = (
        wide_right(
            "sgd,gjfd->gjsf",
            value_local,
            after_state.reshape(group_count, group_size, feat_count, head_dim),
        ).reshape(heads_here, row_count, feat_count)
        + after_norm[:, None, :]
        + wide_left("hrs,hrf->hsf", grad_aff, query_feat)
    )
    grad_wq = wide_right("rhd,hrf->hdf", query_local, grad_qfeat * jax.nn.sigmoid(query_pre))
    grad_wk = wide_right(
        "rgd,gjrf->gjdf",
        key_local,
        (grad_kfeat * jax.nn.sigmoid(key_pre)).reshape(
            group_count, group_size, row_count, feat_count
        ),
    ).reshape(heads_here, head_dim, feat_count)
    return (
        lax.psum(grad_wq.astype(jnp.bfloat16), "seq").astype(jnp.float32),
        lax.psum(grad_wk.astype(jnp.bfloat16), "seq").astype(jnp.float32),
    )


def solution(mesh):
    return jax.shard_map(
        body,
        mesh=mesh,
        in_specs=(
            P("seq", "head"),
            P("seq", "head"),
            P("seq", "head"),
            P("head", None, None),
            P("head", None, None),
        ),
        out_specs=(P("head", None, None), P("head", None, None)),
        check_vma=False,
    )
```

profile of v0, /device:TPU:0, one launch (start us, length us, event | category | flops | bytes accessed | tf_op | source)
XLA Modules:
  0.0 660.6 jit_solution(16312446963119604657)
XLA Ops:
  7.2 1.9 pad_maximum_fusion.1
  11.3 5.7 fusion.99
  17.0 2.0 convolution_convert_fusion
  19.1 6.7 %copy.61 = f32[2,16,384,128]{3,2,1,0:T(8,128)} copy(f32[2,16,384,128]{2,3,1,0:T(8,128)} %get-tuple-element.382) | data formatting | bytes 12582912 | tf_op jit(solution)/shard_map/rgd,gjdf->gjrf/transpose | solution.py:151
  25.8 15.8 %all_gather.16 = bf16[8,32,128]{2,1,0:T(8,128)(2,1)S(1)} all-gather(bf16[1,32,128]{2,1,0:T(8,128)(2,1)S(1)} %bitcast.237), channel_id=1, replica_groups=mesh['seq'=8,'head'=4] {'seq'}, dimensions={0}, use_global_device_ids=true | all-gather | bytes 73728 | tf_op jit(solution)/shard_map/all_gather | solution.py:172
  42.6 3.0 convert_reduce_fusion
  45.6 3.7 select_convert_fusion.1
  51.8 3.5 fusion.32
  55.3 12.1 %select_convert_fusion = (bf16[32,384,384]{1,2,0:T(8,128)(2,1)}, f32[32,384,384]{1,2,0:T(8,128)}) fusion(pred[384,384]{0,1:T(8,128)(4,1)S(1)} %iota_compare_fusion, bf16[32,384,128]{2,1,0:T(8,128)(2,1)S(1)} %select_convert_fusion.1, bf16[32,384,128]{2,1,0:T(8,128)(2,1)S(1)} %fusion.32), kind=kOutput, calls=%fused_computation.50 | convolution fusion | flops 1212678144 | bytes 34750464 | tf_op jit(solution)/shard_map/hrf,hsf->hrs/dot_general | solution.py:185
  67.5 8.1 %select_reduce_fusion = f32[32,384]{1,0:T(8,128)S(1)} fusion(f32[32,384,384]{1,2,0:T(8,128)} %get-tuple-element.381, pred[384,384]{0,1:T(8,128)(4,1)S(1)} %iota_compare_fusion), kind=kLoop, calls=%fused_computation.49 | loop fusion | flops 9424896 | bytes 19070976 | tf_op jit(solution)/shard_map/reduce_sum | solution.py:194
  76.1 8.4 %fusion.81 = f32[2,16,384,128]{2,3,1,0:T(8,128)} fusion(bf16[2,16,384,384]{2,3,1,0:T(8,128)(2,1)} %bitcast.206, bf16[384,2,128,1]{2,1,0,3:T(2,128)(2,1)S(1)} %bitcast.218), kind=kOutput, calls=%fused_computation.130 | convolution fusion | flops 1207959552 | bytes 15925248 | tf_op jit(solution)/shard_map/gjrs,sgd->gjrd/dot_general | solution.py:187
  84.6 2.0 fusion.102
  86.6 2.0 broadcast_in_dim.128
  88.6 2.0 broadcast_in_dim.128.clone
  90.6 72.4 %while.23 = (s32[]{:T(128)}, f32[32,192]{1,0:T(8,128)S(1)}, f32[32,192]{1,0:T(8,128)S(1)}, f32[32,192,128]{2,1,0:T(8,128)}, f32[32,192]{1,0:T(8,128)S(1)}, /*ind...) while((s32[]{:T(128)}, f32[32,192]{1,0:T(8,128)S(1)}, ...), condition=%wide.region_15.16_spmd, body=%wide.region_6.15_spmd.sunk | while | flops 3293799424 | bytes 222832704 | solution.py:139
  91.2 3.3 fusion.134
  95.5 19.5 %conditional.4 = ((f32[32,192]{1,0:T(8,128)S(1)}, f32[32,192]{1,0:T(8,128)S(1)}, f32[32,192,128]{2,1,0:T(8,128)})) conditional(s32[]{:T(128)} %convert_element_type.371, (f32[32,192]{1,0:T(8,128)S(1)}, f32[32,192]{1,0:T(8,128)S(1)}, f32[32,192,128]{2,1,0:T(8,128)}) %tuple.75, (s32[]{:T(128)}, s32[192]{0:T(256)S(1)}, bf16[512,256]{1,0:T(8,128)(2,1)S(1)}, ...), branch_computations={%region_7.7_spmd, %region_8.10_spmd} | conditional | flops 1646899712 | bytes 107746112 | solution.py:130
  95.6 1.8 copy.151
  97.5 2.9 fusion
  100.4 4.2 fusion.4
  104.9 6.3 fusion.5
  111.3 3.7 bitcast_add_fusion
  115.7 19.5 %conditional.5 = ((f32[32,192]{1,0:T(8,128)S(1)}, f32[32,192]{1,0:T(8,128)S(1)}, f32[32,192,128]{2,1,0:T(8,128)})) conditional(s32[]{:T(128)} %convert_element_type.372, (f32[32,192]{1,0:T(8,128)S(1)}, f32[32,192]{1,0:T(8,128)S(1)}, f32[32,192,128]{2,1,0:T(8,128)}) %tuple.77, (s32[]{:T(128)}, s32[192]{0:T(256)S(1)}, ...), branch_computations={%region_11.11_spmd, %region_12.14_spmd} | conditional | flops 1646899712 | bytes 107746112 | solution.py:130
  115.8 1.8 copy.152
  117.7 2.9 fusion.14
  120.6 4.2 fusion.18
  125.2 6.3 fusion.19
  131.5 3.7 bitcast_add_fusion.2
  135.7 3.3 fusion.134
  141.3 3.3 fusion.134
  146.8 3.3 fusion.134
  152.4 3.3 fusion.134
  157.9 3.3 fusion.134
  163.1 5.2 copy.65
  168.2 5.1 copy.64
  173.3 6.7 %divide_convert_fusion = (bf16[32,192,128]{1,2,0:T(8,128)(2,1)}, bf16[32,192,128]{1,2,0:T(8,128)(2,1)}) fusion(f32[32,192,128]{1,2,0:T(8,128)} %copy.65, f32[32,192]{1,0:T(8,128)S(1)} %get-tuple-element.315, f32[32,192,128]{1,2,0:T(8,128)} %copy.64, f32[32,192]{1,0:T(8,128)S(1)} %get-tuple-element.313), kind=kLoop, calls=%fused_computation.85 | loop fusion | flops 3145728 | bytes 9486336 | tf_op jit(solution)/shard_map/convert_element_type | solution.py:142
  180.1 5.8 select_reduce_fusion.1
  185.9 4.1 fusion.75
  190.0 7.5 %multiply_reduce_fusion = (f32[32,384]{1,0:T(8,128)S(1)}, f32[32,384,128]{1,2,0:T(8,128)S(1)}) fusion(bf16[32,192,128]{1,2,0:T(8,128)(2,1)} %get-tuple-element.383, bf16[32,192,128]{1,2,0:T(8,128)(2,1)} %get-tuple-element.384, f32[32,384]{1,0:T(8,128)S(1)} %copy-done.22, f32[2,16,384,128]{2,3,1,0:T(8,128)} %fusion.81, f32[32,384,128]{1,2,0:T(8,128)} %fusion.75, ...), kind=kOutput, calls=%fused_computation.81 | convolution fusion | flops 423612416 | bytes 27361280 | tf_op jit(solution)/shard_map/hrf,hfd->hrd/dot_general | solution.py:41
  197.6 1.4 fusion.45
  200.2 2.4 add_convert_fusion.1
  202.7 6.8 %copy.67 = f32[2,16,384,128]{3,2,1,0:T(8,128)} copy(f32[2,16,384,128]{2,3,1,0:T(8,128)} %bitcast.204) | data formatting | bytes 12582912 | tf_op jit(solution)/shard_map/reshape | solution.py:225
  209.5 11.9 %fusion.64 = f32[2,16,384,384]{3,2,1,0:T(8,128)} fusion(f32[2,16,384,128]{3,2,1,0:T(8,128)} %copy.67, bf16[384,2,128,1]{2,1,0,3:T(2,128)(2,1)S(1)} %bitcast.219), kind=kOutput, calls=%fused_computation.112 | convolution fusion | flops 1209532416 | bytes 25362432 | tf_op jit(solution)/shard_map/gjrd,sgd->gjrs/dot_general | solution.py:34
  221.4 19.1 %convolution_add_fusion = f32[2,16,384,384]{3,2,1,0:T(8,128)} fusion(f32[2,16,384,384]{3,2,1,0:T(8,128)} %fusion.64, f32[2,16,384,128]{3,2,1,0:T(8,128)} %copy.67, bf16[384,2,128,1]{2,1,0,3:T(2,128)(2,1)S(1)} %bitcast.220), kind=kOutput, calls=%fused_computation.55 | convolution fusion | flops 1218969600 | bytes 44236800 | tf_op jit(solution)/shard_map/gjrd,sgd->gjrs/dot_general | solution.py:34
  240.6 18.7 %copy.71 = f32[2,16,384,384]{2,3,1,0:T(8,128)} copy(f32[2,16,384,384]{3,2,1,0:T(8,128)} %convolution_add_fusion) | data formatting | bytes 37748736 | tf_op jit(solution)/shard_map/add | solution.py:34
  259.3 2.7 fusion.91
  262.0 3.1 fusion.89
  265.0 208.5 %all-gather.1 = bf16[256,128]{1,0:T(8,128)(2,1)S(1)} all-gather(bf16[32,128]{1,0:T(8,128)(2,1)S(1)} %add_convert_fusion.3), channel_id=3, replica_groups=mesh['seq'=8,'head'=4] {'seq'}, dimensions={0}, use_global_device_ids=true | all-gather | bytes 73728 | tf_op jit(solution)/shard_map/all_gather | solution.py:218
  473.7 13.8 %fusion.103 = f32[32,384,128]{2,1,0:T(8,128)} fusion(f32[32,384,128]{1,2,0:T(8,128)} %copy-done.7, f32[32,128,128]{2,1,0:T(8,128)S(1)} %select_reduce_fusion.1), kind=kOutput, calls=%fused_computation.163 | convolution fusion | flops 2415919104 | bytes 14680064 | tf_op jit(solution)/shard_map/hrd,hfd->hrf/dot_general | solution.py:230
  487.5 8.3 %subtract_convert_fusion = (bf16[32,384,384]{1,2,0:T(8,128)(2,1)}, bf16[32,384,384]{1,2,0:T(8,128)(2,1)}) fusion(f32[2,16,384,384]{2,3,1,0:T(8,128)S(1)} %copy-done.8, f32[32,384]{1,0:T(8,128)S(1)} %get-tuple-element.357, pred[384,384]{0,1:T(8,128)(4,1)S(1)} %copy-done.18), kind=kLoop, calls=%fused_computation.46 | loop fusion | flops 28311552 | bytes 37945344 | tf_op jit(solution)/shard_map/convert_element_type | solution.py:28
  495.8 9.2 %fusion.104 = f32[32,384,128]{2,1,0:T(8,128)} fusion(bf16[32,384,384]{1,2,0:T(8,128)(2,1)} %get-tuple-element.369, bf16[32,384,128]{2,1,0:T(8,128)(2,1)S(1)} %copy-done.13), kind=kOutput, calls=%fused_computation.164 | convolution fusion | flops 1207959552 | bytes 18874368 | tf_op jit(solution)/shard_map/hrs,hsf->hrf/dot_general | solution.py:34
  505.0 14.6 %divide_multiply_fusion = f32[32,384,128]{2,1,0:T(8,128)} fusion(f32[32,384,128]{2,1,0:T(8,128)} %copy-done.14, f32[32,384,128]{2,1,0:T(8,128)} %fusion.104, f32[32,384,128]{2,1,0:T(8,128)} %fusion.103, f32[32,128]{1,0:T(8,128)S(1)} %copy-done.24, f32[32,384]{1,0:T(8,128)S(1)} %get-tuple-element.357, bf16[32,384,384]{1,2,0:T(8,128)(2,1)} %get-tuple-element.368, ...), kind=kOutput, calls=%fused_computation.79 | convolution fusion | flops 1220542464 | bytes 37814272 | tf_op jit(solution)/shard_map/hrs,hsf->hrf/dot_general | solution.py:34
  519.6 6.2 fusion.44
  525.9 5.1 fusion.66
  531.0 4.5 fusion.105
  535.6 5.8 fusion.29
  542.3 3.7 add_bitcast_fusion
  546.0 6.5 copy.84
  552.6 15.4 %fusion.34 = f32[32,384,128]{2,1,0:T(8,128)} fusion(f32[2,16,384,128]{3,2,1,0:T(8,128)} %copy.84, f32[2,16,384,128]{3,2,1,0:T(8,128)} %copy.61, f32[32,384,128]{2,1,0:T(8,128)} %fusion.105, f32[32,128]{1,0:T(8,128)S(1)} %fusion.80, bf16[32,384,384]{1,2,0:T(8,128)(2,1)} %get-tuple-element.368, bf16[32,384,128]{2,1,0:T(8,128)(2,1)} %copy-done.4), kind=kOutput, calls=%fused_computation.62 | convolution fusion | flops 1218969600 | bytes 37765120 | tf_op jit(solution)/shard_map/hrs,hrf->hsf/dot_general | solution.py:34
  568.0 6.8 %copy.85 = f32[2,16,384,128]{2,3,1,0:T(8,128)} copy(f32[2,16,384,128]{3,2,1,0:T(8,128)} %bitcast.226) | data formatting | bytes 12582912 | tf_op jit(solution)/shard_map/reshape | solution.py:247
  574.8 5.7 fusion.46
  583.5 65.0 %all-reduce.3.cloned.1.call-done = (bf16[32,128,128]{1,2,0:T(8,128)(2,1)}, bf16[32,128,128]{2,1,0:T(8,128)(2,1)}) async-done(((bf16[32,128,128]{1,2,0:T(8,128)(2,1)}, bf16[32,128,128]{2,1,0:T(8,128)(2,1)}), (bf16[32,128,128]{1,2,0:T(8,128)(2,1)}, bf16[32,128,128]{2,1,0:T(8,128)(2,1)})) %all-reduce.3.cloned.1.call-update) | async-done | bytes 2097168 | tf_op jit(solution)/shard_map/psum | solution.py:252
  648.5 2.6 copy.90
  651.1 2.8 convert_element_type.252
  (130 shorter events, 18.8 us)
Async XLA Ops:
  7.2 4.1 copy-start
  7.2 79.4 %all-gather.8.cloned.1.call-start = ((), (), s32[]{:S(2)}) async-start(), calls=%async_computation.1 | async-start | bytes 3538944 | tf_op jit(solution)/shard_map/all_gather | solution.py:103
  9.1 170.9 %all-gather.6.cloned.1.call-start = ((), (), s32[]{:S(2)}) async-start(), calls=%async_computation | async-start | bytes 9437184 | tf_op jit(solution)/shard_map/all_gather | solution.py:169
  10.2 6.8 %copy-start.19 = (bf16[384,2,128]{2,1,0:T(2,128)(2,1)}, bf16[384,2,128]{2,1,0:T(2,128)(2,1)S(1)}, u32[]{:S(2)}) copy-start(bf16[384,2,128]{2,1,0:T(2,128)(2,1)S(1)} %reshape_squeeze_stack.6) | copy-start | bytes 589828
  11.2 64.9 %copy-start.15 = (bf16[384,2,128]{2,1,0:T(2,128)(2,1)}, bf16[384,2,128]{2,1,0:T(2,128)(2,1)S(1)}, u32[]{:S(2)}) copy-start(bf16[384,2,128]{2,1,0:T(2,128)(2,1)S(1)} %reshape_squeeze_stack.7) | copy-start | bytes 589828
  19.0 516.6 %all-gather.10.cloned.1.call-start = ((), (), s32[]{:S(2)}) async-start(), calls=%async_computation.2 | async-start | bytes 9437184 | tf_op jit(solution)/shard_map/all_gather | solution.py:215
  19.0 23.6 %copy-start.21 = (bf16[32,128,128]{2,1,0:T(8,128)(2,1)S(1)}, bf16[32,128,128]{2,1,0:T(8,128)(2,1)}, u32[]{:S(2)}) copy-start(bf16[32,128,128]{2,1,0:T(8,128)(2,1)} %param.14) | copy-start | bytes 3145732
  41.7 0.9 copy-start.25
  41.7 25.7 %copy-start.17 = (pred[384,384]{0,1:T(8,128)(4,1)}, pred[384,384]{0,1:T(8,128)(4,1)S(1)}, u32[]{:S(2)}) copy-start(pred[384,384]{0,1:T(8,128)(4,1)S(1)} %iota_compare_fusion) | copy-start | bytes 442372
  41.8 0.8 copy-start.23
  45.6 5.0 copy-start.14
  45.6 6.2 slice-start.3
  45.6 6.2 slice-start.4
  49.4 5.9 copy-start.4
  55.3 12.2 %copy-start.12 = (bf16[32,384,128]{2,1,0:T(8,128)(2,1)}, bf16[32,384,128]{2,1,0:T(8,128)(2,1)S(1)}, u32[]{:S(2)}) copy-start(bf16[32,384,128]{2,1,0:T(8,128)(2,1)S(1)} %fusion.32) | copy-start | bytes 9437188
  76.1 8.4 %copy-start.10 = (bf16[384,4096]{1,0:T(8,128)(2,1)S(1)}, bf16[384,4096]{1,0:T(8,128)(2,1)}, u32[]{:S(2)}) copy-start(bf16[384,4096]{1,0:T(8,128)(2,1)} %param.11) | copy-start | bytes 9437188
  100.3 4.5 copy-start.2
  120.6 4.5 copy-start.3
  173.3 6.7 %copy-start.26 = (pred[8]{0:T(512)(128)(4,1)S(1)}, pred[8]{0:T(512)(128)(4,1)}, u32[]{:S(2)}) copy-start(pred[8]{0:T(512)(128)(4,1)} %copy-done.25) | copy-start | bytes 28
  180.1 5.9 copy-start.5
  185.9 4.1 copy-start.22
  197.6 2.7 copy-start.7
  202.7 445.8 %all-reduce.3.cloned.1.call-start = ((), (), s32[]{:S(2)}) async-start(), calls=%async_computation.3 | async-start | bytes 4194304 | tf_op jit(solution)/shard_map/psum | solution.py:252
  202.7 6.8 %copy-start.16 = (bf16[384,2,128]{2,1,0:T(2,128)(2,1)S(1)}, bf16[384,2,128]{2,1,0:T(2,128)(2,1)}, u32[]{:S(2)}) copy-start(bf16[384,2,128]{2,1,0:T(2,128)(2,1)} %copy-done.15) | copy-start | bytes 589828
  259.3 228.2 %copy-start.8 = (f32[2,16,384,384]{2,3,1,0:T(8,128)S(1)}, f32[2,16,384,384]{2,3,1,0:T(8,128)}, u32[]{:S(2)}) copy-start(f32[2,16,384,384]{2,3,1,0:T(8,128)} %copy.71) | copy-start | bytes 56623108
  473.7 13.8 %copy-start.18 = (pred[384,384]{0,1:T(8,128)(4,1)S(1)}, pred[384,384]{0,1:T(8,128)(4,1)}, u32[]{:S(2)}) copy-start(pred[384,384]{0,1:T(8,128)(4,1)} %copy-done.17) | copy-start | bytes 442372
  487.5 8.3 %copy-start.13 = (bf16[32,384,128]{2,1,0:T(8,128)(2,1)S(1)}, bf16[32,384,128]{2,1,0:T(8,128)(2,1)}, u32[]{:S(2)}) copy-start(bf16[32,384,128]{2,1,0:T(8,128)(2,1)} %copy-done.12) | copy-start | bytes 9437188
  495.8 9.2 %copy-start.24 = (f32[32,128]{1,0:T(8,128)S(1)}, f32[32,128]{1,0:T(8,128)}, u32[]{:S(2)}) copy-start(f32[32,128]{1,0:T(8,128)} %copy-done.23) | copy-start | bytes 49156
  505.0 14.6 %copy-start.11 = (bf16[384,4096]{1,0:T(8,128)(2,1)S(1)}, bf16[384,4096]{1,0:T(8,128)(2,1)}, u32[]{:S(2)}) copy-start(bf16[384,4096]{1,0:T(8,128)(2,1)} %param.11) | copy-start | bytes 9437188
  519.6 11.4 %slice-start = ((s8[9437184]{0:T(1024)(128)(4,1)}), s8[4194304]{0:T(1024)(128)(4,1)S(1)}, s32[]{:S(2)}) async-start(s8[9437184]{0:T(1024)(128)(4,1)} %bitcast.202), calls=%async_computation.4 | async-start | bytes 8388608
  519.6 11.4 %slice-start.1 = ((s8[9437184]{0:T(1024)(128)(4,1)}), s8[4194304]{0:T(1024)(128)(4,1)S(1)}, s32[]{:S(2)}) async-start(s8[9437184]{0:T(1024)(128)(4,1)} %bitcast.202), calls=%async_computation.5 | async-start | bytes 8388608
  525.9 5.2 copy-start.6
  525.9 5.2 slice-start.2
  568.0 6.8 %copy-start.20 = (bf16[384,2,128]{2,1,0:T(2,128)(2,1)S(1)}, bf16[384,2,128]{2,1,0:T(2,128)(2,1)}, u32[]{:S(2)}) copy-start(bf16[384,2,128]{2,1,0:T(2,128)(2,1)} %copy-done.19) | copy-start | bytes 589828
  574.8 6.4 copy-start.9
  581.2 72.7 %copy-start.1 = (bf16[32,128,128]{2,1,0:T(8,128)(2,1)S(1)}, bf16[32,128,128]{2,1,0:T(8,128)(2,1)}, u32[]{:S(2)}) copy-start(bf16[32,128,128]{2,1,0:T(8,128)(2,1)} %param.15) | copy-start | bytes 3145732
Sparse Core Ops, SparseCore 0:
  9.6 41.5 all-gather.7
  52.8 80.9 all-gather.5
  202.8 276.7 all-gather.9
  583.6 64.8 all-reduce.2
where the time goes:
time: 666 us; the launch traced here: 661 us
  blocking collectives  224 us (34%)
  matrix products  184 us (28%)
  local copies, waits for them, and re-layouts  99.8 us (15%)
  waiting for transfers between devices  65 us (10%)
  other arithmetic  64.3 us (10%)
  between operations  14.4 us (2%)
  loops' own time  8.05 us (1%)
    all_gather x1, blocking collectives, body(): lax.all_gather(back_norm[None].astype(jnp.bfloat16), 'seq', axis=0, tiled...  209 us
    psum x1, waiting for transfers between devices, body(): lax.psum(grad_wq.astype(jnp.bfloat16), 'seq').astype(jnp.float32)  65 us
    dot_general x3, matrix products, wide_left(): jnp.einsum(form, low, narrow, preferred_element_type=jnp.float32)  49.1 us
    dot_general x7, matrix products, wide_right(): jnp.einsum(form, narrow, low, preferred_element_type=jnp.float32)  28.9 us
    dot_general x3, matrix products, wide_left(): jnp.einsum(form, high, narrow, preferred_element_type=jnp.float32)  25.6 us
    slice x6, local copies, waits for them, and re-layouts, one_step(): value_rows = lax.dynamic_slice_in_dim(shard_part[1], offset, block_rows, 0)  19.6 us
    add x1, local copies, waits for them, and re-layouts, wide_left(): jnp.einsum(form, high, narrow, preferred_element_type=jnp.float32)  18.7 us
    dot_general x7, matrix products, wide_right(): jnp.einsum(form, narrow, high, preferred_element_type=jnp.float32)  17.5 us
  transfers between devices with their start and end apart: 4, of which 1 were waited for; matrix products, arithmetic and copies ran while one was open for 41% of the time, Pallas kernels for 0%

commit v1 on v0

v1 whole, which is shorter than its diff:
```python
import functools
import math

import jax
import jax.numpy as jnp
from jax import lax
from jax.experimental import pallas as pl
from jax.experimental.pallas import tpu as pltpu
from jax.sharding import PartitionSpec as P

HEADS = 128
KV_HEADS = 8
CORES = 2
LOG2E = math.log2(math.e)
MASKED_SCORE = -1e30
VMEM_BYTES = 48 * 1024 * 1024
F32 = jnp.float32
BF16 = jnp.bfloat16

NN = (((1,), (0,)), ((), ()))
NT = (((1,), (1,)), ((), ()))
TN = (((0,), (0,)), ((), ()))


def dot(a, b, form):
    return lax.dot_general(a, b, form, preferred_element_type=F32)


def from_partner(block, axis, stride):
    count = lax.axis_size(axis)
    route = []
    for low in range(count):
        high = low | 1 << stride
        if high != low and high < count:
            route += [(low, high), (high, low)]
    return lax.ppermute(block, axis, route)


def tile_of(rows):
    return 256 if rows % 256 == 0 else rows


def with_ones(values):
    return jnp.concatenate((values, jnp.ones_like(values)), axis=1)


def log1p_exp(decay):
    return jnp.where(decay < 0.01, decay - 0.5 * decay * decay, jnp.log(1.0 + decay))


def features(pre):
    decay = jnp.exp(-jnp.abs(pre))
    return (jnp.maximum(pre, 0.0) + log1p_exp(decay)).astype(BF16)


def slope(pre):
    decay = jnp.exp(-jnp.abs(pre))
    inverse = 1.0 / (1.0 + decay)
    return jnp.where(pre >= 0, inverse, decay * inverse)


def causal_mask(rows):
    return lax.broadcasted_iota(jnp.int32, (rows, rows), 0) >= lax.broadcasted_iota(
        jnp.int32, (rows, rows), 1
    )


def local_attention(scale, q_ref, k_ref, v_ref, acc_ref, stat_ref):
    head = pl.program_id(0)
    rows, width = q_ref.shape
    tile = tile_of(rows)
    lane = lax.broadcasted_iota(jnp.int32, (tile, stat_ref.shape[1]), 1)
    mask = causal_mask(tile)
    wide = with_ones(v_ref[...])
    for i in range(rows // tile):
        here = pl.ds(i * tile, tile)
        end = (i + 1) * tile
        scores = dot(q_ref[here, :], k_ref[:end, :], NT) * scale
        last = jnp.where(mask, scores[:, end - tile :], MASKED_SCORE)
        scores = last if i == 0 else jnp.concatenate((scores[:, : end - tile], last), axis=1)
        peak = jnp.max(scores, axis=1, keepdims=True)
        mixed = dot(jnp.exp2(scores - peak).astype(BF16), wide[:end], NN)
        acc_ref[here, :] = mixed[:, :width]
        stat = jnp.where(lane == head, peak, stat_ref[here, :])
        stat_ref[here, :] = jnp.where(lane == head + 64, mixed[:, width : width + 1], stat)


def chunk_attention(
    scale,
    distance,
    place_ref,
    q_ref,
    k_ref,
    v_ref,
    wk_ref,
    acc_in,
    stat_in,
    state_in,
    acc_ref,
    stat_ref,
    state_ref,
):
    head = pl.program_id(0)
    rows, width = q_ref.shape
    tile = tile_of(rows)
    lane = lax.broadcasted_iota(jnp.int32, (tile, stat_ref.shape[1]), 1)

    @pl.when(head == 0)
    def _():
        stat_ref[...] = stat_in[...]

    @pl.when(place_ref[0] < distance)
    def _():
        acc_ref[...] = acc_in[...]
        state_ref[...] = state_in[...]

    @pl.when(place_ref[0] >= distance)
    def _():
        wide = with_ones(v_ref[...])
        for i in range(rows // tile):
            here = pl.ds(i * tile, tile)
            scores = dot(q_ref[here, :], k_ref[...], NT) * scale
            stat = stat_ref[here, :]
            old_peak = jnp.sum(jnp.where(lane == head, stat, 0.0), axis=1, keepdims=True)
            old_sum = jnp.sum(jnp.where(lane == head + 64, stat, 0.0), axis=1, keepdims=True)
            peak = jnp.maximum(jnp.max(scores, axis=1, keepdims=True), old_peak)
            mixed = dot(jnp.exp2(scores - peak).astype(BF16), wide, NN)
            factor = jnp.exp2(old_peak - peak)
            acc_ref[here, :] = acc_in[here, :] * factor + mixed[:, :width]
            stat = jnp.where(lane == head, peak, stat)
            stat_ref[here, :] = jnp.where(
                lane == head + 64, old_sum * factor + mixed[:, width : width + 1], stat
            )
        key_feat = features(dot(k_ref[...], wk_ref[0], NN))
        state_ref[0] = state_in[0] + dot(key_feat, wide, TN)


def student(total_tokens, chunk_count, place_ref, q_ref, k_ref, v_ref, *refs):
    chunk_refs = refs[: 2 * chunk_count]
    wq_ref, wk_ref, acc_ref, stat_ref, state_ref, out_ref, wk_acc = refs[2 * chunk_count :]
    head = pl.program_id(0) + place_ref[1]
    rows, width = q_ref.shape
    tile = tile_of(rows)
    tiles = rows // tile
    lane = lax.broadcasted_iota(jnp.int32, (tile, stat_ref.shape[1]), 1)
    mask = causal_mask(tile)
    state = state_ref[0]
    query_pre, key_pre, key_feat, query_feat, wide, states, grads, backs = ([] for _ in range(8))
    for i in range(tiles):
        here = pl.ds(i * tile, tile)
        query_pre.append(dot(q_ref[here, :], wq_ref[0], NN))
        key_pre.append(dot(k_ref[here, :], wk_ref[0], NN))
        query_feat.append(features(query_pre[i]))
        key_feat.append(features(key_pre[i]))
        wide.append(with_ones(v_ref[here, :]))
        affinity = jnp.where(mask, dot(query_feat[i], key_feat[i], NT), 0.0).astype(BF16)
        states.append(state.astype(BF16))
        mixed = dot(affinity, wide[i], NN) + dot(query_feat[i], states[i], NN)
        inverse = 1.0 / mixed[:, width:]
        result = mixed[:, :width] * inverse
        stat = stat_ref[here, :]
        total = jnp.sum(jnp.where(lane == head + 64, stat, 0.0), axis=1, keepdims=True)
        teacher = (acc_ref[here, :] / total).astype(BF16).astype(F32)
        grad_out = (result - teacher) * (2.0 / total_tokens)
        grad_numer = grad_out * inverse
        grad_denom = jnp.sum(grad_out * result, axis=1, keepdims=True) * inverse * (-1.0 / width)
        grads.append(jnp.concatenate((grad_numer, grad_denom), axis=1).astype(BF16))
        backs.append(dot(query_feat[i], grads[i], TN))
        state = state + dot(key_feat[i], wide[i], TN)
    after = jnp.zeros_like(state)
    grad_wq = jnp.zeros(wq_ref.shape[1:], F32)
    grad_wk = jnp.zeros(wk_ref.shape[1:], F32)
    for i in reversed(range(tiles)):
        here = pl.ds(i * tile, tile)
        grad_aff = jnp.where(mask, dot(grads[i], wide[i], NT), 0.0).astype(BF16)
        grad_qfeat = dot(grads[i], states[i], NT) + dot(grad_aff, key_feat[i], NN)
        grad_kfeat = dot(grad_aff, query_feat[i], TN)
        if i < tiles - 1:
            grad_kfeat = grad_kfeat + dot(wide[i], after.astype(BF16), NT)
        after = after + backs[i]
        grad_wq += dot(q_ref[here, :], (grad_qfeat * slope(query_pre[i])).astype(BF16), TN)
        grad_wk += dot(k_ref[here, :], (grad_kfeat * slope(key_pre[i])).astype(BF16), TN)
    out_ref[0, 0] = grad_wq.astype(out_ref.dtype)
    wk_acc[...] = grad_wk
    after = after.astype(BF16)
    for c in range(chunk_count):

        @pl.when(place_ref[0] >= c + 1)
        def _(c=c):
            keys = chunk_refs[2 * c][...]
            grad_kfeat = dot(with_ones(chunk_refs[2 * c + 1][...]), after, NT)
            change = grad_kfeat * slope(dot(keys, wk_ref[0], NN))
            wk_acc[...] += dot(keys, change.astype(BF16), TN)

    out_ref[0, 1] = wk_acc[...].astype(out_ref.dtype)


def params():
    return pltpu.CompilerParams(
        vmem_limit_bytes=VMEM_BYTES, dimension_semantics=("arbitrary",)
    )


def body(queries, keys, values, feat_q, feat_k):
    row_count = queries.shape[0]
    heads_here, head_dim, feat_count = feat_q.shape
    seq_count = lax.axis_size("seq")
    chips = seq_count // CORES
    seq_place = lax.axis_index("seq")
    core, chip = seq_place % CORES, seq_place // CORES
    head_place = lax.axis_index("head")
    spread = max(1, HEADS // KV_HEADS // heads_here)
    key_value = jnp.stack((keys, values))
    for bit_index in range(spread.bit_length() - 1):
        partner = from_partner(key_value, "head", bit_index)
        upper_half = head_place // (1 << bit_index) % 2 == 1
        key_value = jnp.where(
            upper_half,
            jnp.concatenate((partner, key_value), axis=2),
            jnp.concatenate((key_value, partner), axis=2),
        )
    groups = key_value.shape[2] // head_dim
    half = heads_here // CORES
    core_route = [(i, i ^ 1) for i in range(seq_count)]
    first = core == 0

    def pair_up(low, high, axis):
        mine = jnp.where(first, low, high)
        other = lax.ppermute(jnp.where(first, high, low), "seq", core_route)
        return jnp.where(
            first,
            jnp.concatenate((mine, other), axis=axis),
            jnp.concatenate((other, mine), axis=axis),
        )

    if groups > 1:
        own_groups = groups // CORES
        split = own_groups * head_dim
        kv = pair_up(key_value[:, :, :split], key_value[:, :, split:], 1)
    else:
        own_groups = groups
        kv = pair_up(key_value, key_value, 1)
    kv = jnp.concatenate((kv[0], kv[1]), axis=1)
    q = pair_up(queries[:, : half * head_dim], queries[:, half * head_dim :], 0)
    rows = CORES * row_count
    up_route = [(i, i + CORES) for i in range(seq_count - CORES)]
    chunks = []
    for _ in range(chips - 1):
        chunks.append(lax.ppermute(chunks[-1] if chunks else kv, "seq", up_route))
    wk = lax.dynamic_slice_in_dim(feat_k, core * half, half, 0)
    wq = lax.dynamic_slice_in_dim(feat_q, core * half, half, 0)

    per_group = half // own_groups
    scale = head_dim ** (-0.5) * LOG2E
    q_spec = pl.BlockSpec((rows, head_dim), lambda h, *_: (0, h))
    k_spec = pl.BlockSpec((rows, head_dim), lambda h, *_: (0, h // per_group))
    v_spec = pl.BlockSpec((rows, head_dim), lambda h, *_: (0, own_groups + h // per_group))
    stat_spec = pl.BlockSpec((rows, 128), lambda h, *_: (0, 0))
    w_spec = pl.BlockSpec((1, head_dim, feat_count), lambda h, *_: (h, 0, 0))
    state_spec = pl.BlockSpec((1, feat_count, 2 * head_dim), lambda h, *_: (h, 0, 0))
    acc_type = jax.ShapeDtypeStruct((rows, half * head_dim), F32)
    stat_type = jax.ShapeDtypeStruct((rows, 128), F32)
    state_type = jax.ShapeDtypeStruct((half, feat_count, 2 * head_dim), F32)

    acc, stat = pl.pallas_call(
        functools.partial(local_attention, scale),
        grid=(half,),
        in_specs=[q_spec, k_spec, v_spec],
        out_specs=[q_spec, stat_spec],
        out_shape=[acc_type, stat_type],
        compiler_params=params(),
        name="local_attention",
    )(q, kv, kv)
    state = jnp.zeros(state_type.shape, F32)
    place = jnp.stack((chip, jnp.zeros_like(chip))).astype(jnp.int32)
    for index, chunk in enumerate(chunks):
        acc, stat, state = pl.pallas_call(
            functools.partial(chunk_attention, scale, index + 1),
            grid_spec=pltpu.PrefetchScalarGridSpec(
                num_scalar_prefetch=1,
                grid=(half,),
                in_specs=[q_spec, k_spec, v_spec, w_spec, q_spec, stat_spec, state_spec],
                out_specs=[q_spec, stat_spec, state_spec],
            ),
            out_shape=[acc_type, stat_type, state_type],
            input_output_aliases={5: 0, 6: 1, 7: 2},
            compiler_params=params(),
            name="chunk_attention",
        )(place, q, chunk, chunk, wk, acc, stat, state)

    grads = pl.pallas_call(
        functools.partial(student, row_count * seq_count, len(chunks)),
        grid_spec=pltpu.PrefetchScalarGridSpec(
            num_scalar_prefetch=1,
            grid=(half,),
            in_specs=[q_spec, k_spec, v_spec]
            + [k_spec, v_spec] * len(chunks)
            + [w_spec, w_spec, q_spec, stat_spec, state_spec],
            out_specs=pl.BlockSpec((1, 2, head_dim, feat_count), lambda h, *_: (h, 0, 0, 0)),
            scratch_shapes=[pltpu.VMEM((head_dim, feat_count), F32)],
        ),
        out_shape=jax.ShapeDtypeStruct((half, 2, head_dim, feat_count), BF16),
        compiler_params=params(),
        name="student",
    )(place, q, kv, kv, *[c for chunk in chunks for c in (chunk, chunk)], wq, wk, acc, stat, state)

    flat = grads.reshape(-1, feat_count)
    share = flat.shape[0] // chips

    def shift_route(distance):
        return [(i, (i + CORES * distance) % seq_count) for i in range(seq_count)]

    def part(index):
        return lax.dynamic_slice_in_dim(flat, index % chips * share, share, 0)

    mine = part(chip).astype(F32)
    for distance in range(1, chips):
        mine += lax.ppermute(part(chip + distance), "seq", shift_route(distance)).astype(F32)
    mine = mine.astype(BF16)
    whole = lax.dynamic_update_slice_in_dim(jnp.zeros_like(flat), mine, chip * share, 0)
    for distance in range(1, chips):
        got = lax.ppermute(mine, "seq", shift_route(distance))
        whole = lax.dynamic_update_slice_in_dim(
            whole, got, (chip - distance + chips) % chips * share, 0
        )
    whole = whole.reshape(half, 2, head_dim, feat_count)
    other = lax.ppermute(whole, "seq", core_route)
    both = jnp.where(
        first, jnp.concatenate((whole, other), axis=0), jnp.concatenate((other, whole), axis=0)
    ).astype(F32)
    return both[:, 0], both[:, 1]


def solution(mesh):
    return jax.shard_map(
        body,
        mesh=mesh,
        in_specs=(
            P("seq", "head"),
            P("seq", "head"),
            P("seq", "head"),
            P("head", None, None),
            P("head", None, None),
        ),
        out_specs=(P("head", None, None), P("head", None, None)),
        check_vma=False,
    )
```

time: 666 us -> 275 us (0.41)
  blocking collectives: 224 us -> 0 us
  matrix products: 184 us -> 0 us
  Pallas kernels: 0 us -> 117 us
  local copies, waits for them, and re-layouts: 99.8 us -> 4.34 us
  starting transfers between devices: 0.16 us -> 92.4 us
  other arithmetic: 64.3 us -> 8.22 us
  waiting for transfers between devices: 65 us -> 47.4 us
  between operations: 14.4 us -> 0.88 us
  loops' own time: 8.05 us -> 0 us
    all_gather x2 -> x0, blocking collectives: 224 us -> none  [the longest x1 209 us: body(): lax.all_gather(back_norm[None].astype(jnp.bfloat16), 'seq', axis=0, tiled...]
    dot_general x30 -> x0, matrix products: 184 us -> none  [the longest x3 49.1 us: wide_left(): jnp.einsum(form, low, narrow, preferred_element_type=jnp.float32)]
    pallas_call x0 -> x5, Pallas kernels: none -> 117 us  [the longest x1 56 us: body(): pl.pallas_call(functools.partial(student, row_count * seq_count, len(chun...]
    ppermute x0 -> x12, starting transfers between devices: none -> 92.4 us  [the longest x3 63.8 us: body(): lax.ppermute(part(chip + distance), 'seq', shift_route(distance))]
    psum x1 -> x0, waiting for transfers between devices: 65 us -> none  [body(): lax.psum(grad_wq.astype(jnp.bfloat16), 'seq').astype(jnp.float32)]
    ppermute x0 -> x12, waiting for transfers between devices: none -> 47.4 us  [the longest x3 15.5 us: body(): lax.ppermute(part(chip + distance), 'seq', shift_route(distance))]
    reduce_sum x7 -> x0, other arithmetic: 28.2 us -> none  [the longest x2 8.39 us: attend_block(): row_total = row_total * factor + jnp.sum(weights, axis=-1)]
    add x2 -> x0, local copies, waits for them, and re-layouts: 25.2 us -> none  [the longest x1 18.7 us: wide_left(): jnp.einsum(form, high, narrow, preferred_element_type=jnp.float32)]
  transfers between devices with their start and end apart: 4 -> 12, of which waited for: 1 -> 8; matrix products, arithmetic and copies ran while one was open for 41% -> 3% of each run, Pallas kernels for 0% -> 18%
where the time goes in v1:
time: 275 us; the launch traced here: 270 us
  Pallas kernels  117 us (43%)
  starting transfers between devices  92.4 us (34%)
  waiting for transfers between devices  47.4 us (17%)
  other arithmetic  8.22 us (3%)
  local copies, waits for them, and re-layouts  4.34 us (2%)
    ppermute x3, starting transfers between devices, body(): lax.ppermute(part(chip + distance), 'seq', shift_route(distance))  63.8 us
    pallas_call x1, Pallas kernels, body(): pl.pallas_call(functools.partial(student, row_count * seq_count, len(chun...  56 us
    pallas_call x3, Pallas kernels, body(): pl.pallas_call(functools.partial(chunk_attention, scale, index + 1), grid...  37.7 us
    pallas_call x1, Pallas kernels, body(): pl.pallas_call(functools.partial(local_attention, scale), grid=(half,), i...  23.1 us
    ppermute x3, waiting for transfers between devices, body(): lax.ppermute(part(chip + distance), 'seq', shift_route(distance))  15.5 us
    ppermute x3, waiting for transfers between devices, body(): chunks.append(lax.ppermute(chunks[-1] if chunks else kv, 'seq', up_route))  14.8 us
    ppermute x3, waiting for transfers between devices, body(): got = lax.ppermute(mine, 'seq', shift_route(distance))  14.5 us
    ppermute x3, starting transfers between devices, body(): got = lax.ppermute(mine, 'seq', shift_route(distance))  14.2 us
  transfers between devices with their start and end apart: 12, of which 8 were waited for; matrix products, arithmetic and copies ran while one was open for 3% of the time, Pallas kernels for 18%

profile of v1, /device:TPU:0, one launch (start us, length us, event | category | flops | bytes accessed | tf_op | source)
XLA Modules:
  0.0 270.1 jit_solution(4869396225992890782)
XLA Ops:
  0.6 1.2 broadcast_select_fusion.3
  1.9 0.5 collective-permute-start.1
  2.4 3.2 %broadcast_select_fusion.1 = (bf16[384,2048]{1,0:T(8,128)(2,1)S(1)}, bf16[384,2048]{1,0:T(8,128)(2,1)}) fusion(pred[]{:T(512)S(6)} %eq.12, bf16[384,4096]{1,0:T(8,128)(2,1)} %param.5), kind=kLoop, calls=%fused_computation.6 | loop fusion | flops 1572864 | bytes 6291457 | tf_op jit(solution)/shard_map/jit(_where)/select_n | solution.py:228
  5.6 0.1 collective-permute-start
  5.7 0.0 collective-permute-done.1
  5.7 0.1 maximum_select_fusion.2
  5.9 5.0 %collective-permute-start.2 = (bf16[768,256]{1,0:T(8,128)(2,1)S(1)}, bf16[768,256]{1,0:T(8,128)(2,1)S(1)}, u32[]{:S(2)}, u32[]{:S(2)}) collective-permute-start(bf16[768,256]{1,0:T(8,128)(2,1)S(1)} %pad_maximum_fusion.k_ref.v_ref), channel_id=1, source_target_pairs={{0,8},{4,12},{8,16},{12,20},{16,24},{20,28},{1,9},{5,13},{9,17},{1... | collective-permute-start | bytes 1179656 | tf_op jit(solution)/shard_map/ppermute | solution.py:249
  10.8 8.5 %collective-permute-done.2.k_ref.v_ref.refs_0_.refs_1_ = bf16[768,256]{1,0:T(8,128)(2,1)S(1)} collective-permute-done((bf16[768,256]{1,0:T(8,128)(2,1)S(1)}, bf16[768,256]{1,0:T(8,128)(2,1)S(1)}, u32[]{:S(2)}, u32[]{:S(2)}) %collective-permute-start.2) | collective-permute-done | bytes 393248 | tf_op jit(solution)/shard_map/ppermute | solution.py:249
  19.4 4.4 %collective-permute-start.3 = (bf16[768,256]{1,0:T(8,128)(2,1)S(1)}, bf16[768,256]{1,0:T(8,128)(2,1)S(1)}, u32[]{:S(2)}, u32[]{:S(2)}) collective-permute-start(bf16[768,256]{1,0:T(8,128)(2,1)S(1)} %collective-permute-done.2.k_ref.v_ref.refs_0_.refs_1_), channel_id=1, source_target_pairs={{0,8},{4,12},{8,16},{12,20},{16,24},{20,28},{1,9},{5,13},{9,17},{1... | collective-permute-start | bytes 1179656 | tf_op jit(solution)/shard_map/ppermute | solution.py:249
  23.8 1.3 constant_dynamic-slice_fusion.3
  25.2 6.3 %collective-permute-done.3.k_ref.v_ref.refs_2_.refs_3_ = bf16[768,256]{1,0:T(8,128)(2,1)S(1)} collective-permute-done((bf16[768,256]{1,0:T(8,128)(2,1)S(1)}, bf16[768,256]{1,0:T(8,128)(2,1)S(1)}, u32[]{:S(2)}, u32[]{:S(2)}) %collective-permute-start.3) | collective-permute-done | bytes 393248 | tf_op jit(solution)/shard_map/ppermute | solution.py:249
  31.4 4.4 %collective-permute-start.4 = (bf16[768,256]{1,0:T(8,128)(2,1)S(1)}, bf16[768,256]{1,0:T(8,128)(2,1)S(1)}, u32[]{:S(2)}, u32[]{:S(2)}) collective-permute-start(bf16[768,256]{1,0:T(8,128)(2,1)S(1)} %collective-permute-done.3.k_ref.v_ref.refs_2_.refs_3_), channel_id=1, source_target_pairs={{0,8},{4,12},{8,16},{12,20},{16,24},{20,28},{1,9},{5,13},{9,17},{1... | collective-permute-start | bytes 1179656 | tf_op jit(solution)/shard_map/ppermute | solution.py:249
  35.8 0.1 pad_add_fusion.place_ref
  35.9 0.0 collective-permute-done
  35.9 3.0 %maximum_select_fusion.q_ref = bf16[768,2048]{1,0:T(8,128)(2,1)S(1)} fusion(bf16[384,2048]{1,0:T(8,128)(2,1)} %collective-permute-done, bf16[384,2048]{1,0:T(8,128)(2,1)S(1)} %get-tuple-element.28, pred[]{:T(512)S(6)} %eq.12), kind=kLoop, calls=%fused_computation | loop fusion | flops 14155776 | bytes 6291457 | tf_op jit(solution)/shard_map/jit(_where)/select_n | solution.py:230
  38.9 0.0 copy-start
  38.9 23.1 %local_attention.1 = (f32[768,2048]{1,0:T(8,128)}, f32[768,128]{1,0:T(8,128)S(1)}) custom-call(bf16[768,2048]{1,0:T(8,128)(2,1)S(1)} %maximum_select_fusion.q_ref, bf16[768,256]{1,0:T(8,128)(2,1)S(1)} %pad_maximum_fusion.k_ref.v_ref, bf16[768,256]{1,0:T(8,128)(2,1)S(1)} %pad_maximum_fusion.k_ref.v_ref), custom_call_target="tpu_custom_call" | custom-call | tf_op jit(solution)/shard_map/local_attention/pallas_call | solution.py:265
  62.0 0.2 broadcast_in_dim.7.state_in
  62.2 0.0 copy-done
  62.3 12.6 %chunk_attention.3 = (f32[768,2048]{1,0:T(8,128)}, f32[768,128]{1,0:T(8,128)S(1)}, f32[16,128,256]{2,1,0:T(8,128)S(1)}) custom-call(s32[2]{0:T(128)S(1)} %pad_add_fusion.place_ref, bf16[768,2048]{1,0:T(8,128)(2,1)} %copy-done, ...), custom_call_target="tpu_custom_call", output_to_operand_aliasing={{0}: (5, {}), {1}: (6, {}), {2}: (7, {})} | custom-call | tf_op jit(solution)/shard_map/chunk_attention/pallas_call | solution.py:277
  74.8 12.6 %chunk_attention.4 = (f32[768,2048]{1,0:T(8,128)}, f32[768,128]{1,0:T(8,128)S(1)}, f32[16,128,256]{2,1,0:T(8,128)S(1)}) custom-call(s32[2]{0:T(128)S(1)} %pad_add_fusion.place_ref, bf16[768,2048]{1,0:T(8,128)(2,1)} %copy-done, ...), custom_call_target="tpu_custom_call", output_to_operand_aliasing={{0}: (5, {}), {1}: (6, {}), {2}: (7, {})} | custom-call | tf_op jit(solution)/shard_map/chunk_attention/pallas_call | solution.py:277
  87.4 0.0 collective-permute-done.4.k_ref.v_ref.refs_4_.refs_5_
  87.4 12.6 %chunk_attention.5 = (f32[768,2048]{1,0:T(8,128)}, f32[768,128]{1,0:T(8,128)S(1)}, f32[16,128,256]{2,1,0:T(8,128)S(1)}) custom-call(s32[2]{0:T(128)S(1)} %pad_add_fusion.place_ref, bf16[768,2048]{1,0:T(8,128)(2,1)} %copy-done, ...), custom_call_target="tpu_custom_call", output_to_operand_aliasing={{0}: (5, {}), {1}: (6, {}), {2}: (7, {})} | custom-call | tf_op jit(solution)/shard_map/chunk_attention/pallas_call | solution.py:277
  100.0 56.0 %student.1 = bf16[16,2,128,128]{3,2,1,0:T(8,128)(2,1)S(1)} custom-call(s32[2]{0:T(128)S(1)} %pad_add_fusion.place_ref, bf16[768,2048]{1,0:T(8,128)(2,1)} %copy-done, bf16[768,256]{1,0:T(8,128)(2,1)S(1)} %pad_maximum_fusion.k_ref.v_ref, bf16[768,256]{1,0:T(8,128)(2,1)S(1)} %pad_maximum_fusion.k_ref.v_ref, ...), custom_call_target="tpu_custom_call" | custom-call | tf_op jit(solution)/shard_map/student/pallas_call | solution.py:291
  155.9 0.1 constant_dynamic-slice_fusion.2
  156.0 22.3 %collective-permute-start.5 = (bf16[1024,128]{1,0:T(8,128)(2,1)S(1)}, bf16[1024,128]{1,0:T(8,128)(2,1)S(1)}, u32[]{:S(2)}, u32[]{:S(2)}) collective-permute-start(bf16[1024,128]{1,0:T(8,128)(2,1)S(1)} %get-tuple-element.30), channel_id=1, source_target_pairs={{0,8},{4,12},{8,16},{12,20},{16,24},{20,28},{24,0},{28,4},{1,9},{5... | collective-permute-start | bytes 786440 | tf_op jit(solution)/shard_map/ppermute | solution.py:318
  178.3 41.5 %collective-permute-start.6 = (bf16[1024,128]{1,0:T(8,128)(2,1)S(1)}, bf16[1024,128]{1,0:T(8,128)(2,1)S(1)}, u32[]{:S(2)}, u32[]{:S(2)}) collective-permute-start(bf16[1024,128]{1,0:T(8,128)(2,1)S(1)} %get-tuple-element.32), channel_id=1, source_target_pairs={{0,16},{4,20},{8,24},{12,28},{16,0},{20,4},{24,8},{28,12},{1,17},{... | collective-permute-start | bytes 786440 | tf_op jit(solution)/shard_map/ppermute | solution.py:318
  219.8 0.0 collective-permute-start.7
  219.8 6.7 %collective-permute-done.5 = bf16[1024,128]{1,0:T(8,128)(2,1)S(1)} collective-permute-done((bf16[1024,128]{1,0:T(8,128)(2,1)S(1)}, bf16[1024,128]{1,0:T(8,128)(2,1)S(1)}, u32[]{:S(2)}, u32[]{:S(2)}) %collective-permute-start.5) | collective-permute-done | bytes 262176 | tf_op jit(solution)/shard_map/ppermute | solution.py:318
  226.6 8.8 %collective-permute-done.6 = bf16[1024,128]{1,0:T(8,128)(2,1)S(1)} collective-permute-done((bf16[1024,128]{1,0:T(8,128)(2,1)S(1)}, bf16[1024,128]{1,0:T(8,128)(2,1)S(1)}, u32[]{:S(2)}, u32[]{:S(2)}) %collective-permute-start.6) | collective-permute-done | bytes 262176 | tf_op jit(solution)/shard_map/ppermute | solution.py:318
  235.3 0.0 collective-permute-done.7
  235.3 0.1 broadcast_in_dim.6
  235.5 0.2 constant_dynamic-update-slice_fusion.3
  235.7 11.8 %collective-permute-start.8 = (bf16[1024,128]{1,0:T(8,128)(2,1)S(1)}, bf16[1024,128]{1,0:T(8,128)(2,1)S(1)}, u32[]{:S(2)}, u32[]{:S(2)}) collective-permute-start(bf16[1024,128]{1,0:T(8,128)(2,1)S(1)} %get-tuple-element.25), channel_id=1, source_target_pairs={{0,8},{4,12},{8,16},{12,20},{16,24},{20,28},{24,0},{28,4},{1,9},{5... | collective-permute-start | bytes 786440 | tf_op jit(solution)/shard_map/ppermute | solution.py:322
  247.4 0.0 collective-permute-start.9
  247.4 2.4 collective-permute-start.10
  249.8 4.2 %collective-permute-done.8 = bf16[1024,128]{1,0:T(8,128)(2,1)S(1)} collective-permute-done((bf16[1024,128]{1,0:T(8,128)(2,1)S(1)}, bf16[1024,128]{1,0:T(8,128)(2,1)S(1)}, u32[]{:S(2)}, u32[]{:S(2)}) %collective-permute-start.8) | collective-permute-done | bytes 262176 | tf_op jit(solution)/shard_map/ppermute | solution.py:322
  254.1 7.6 %collective-permute-done.9 = bf16[1024,128]{1,0:T(8,128)(2,1)S(1)} collective-permute-done((bf16[1024,128]{1,0:T(8,128)(2,1)S(1)}, bf16[1024,128]{1,0:T(8,128)(2,1)S(1)}, u32[]{:S(2)}, u32[]{:S(2)}) %collective-permute-start.9) | collective-permute-done | bytes 262176 | tf_op jit(solution)/shard_map/ppermute | solution.py:322
  261.8 2.6 collective-permute-done.10
  264.5 0.1 collective-permute-start.11
  264.6 2.6 collective-permute-done.11
  267.2 0.4 fusion
  267.6 2.5 slice_bitcast_fusion
  (5 shorter events, 0.2 us)
Async XLA Ops:
  1.9 3.8 %collective-permute-start.1 = (bf16[2,384,128]{2,1,0:T(8,128)(2,1)S(1)}, bf16[2,384,128]{2,1,0:T(8,128)(2,1)S(1)}, u32[]{:S(2)}, u32[]{:S(2)}) collective-permute-start(bf16[2,384,128]{2,1,0:T(8,128)(2,1)S(1)} %get-tuple-element.36), channel_id=1, source_target_pairs={{0,4},{4,0},{8,12},{12,8},{16,20},{20,16},{24,28},{28,24},{1,5},{5... | collective-permute-start | bytes 589832 | tf_op jit(solution)/shard_map/ppermute | solution.py:229
  5.6 30.3 %collective-permute-start = (bf16[384,2048]{1,0:T(8,128)(2,1)}, bf16[384,2048]{1,0:T(8,128)(2,1)}, u32[]{:S(2)}, u32[]{:S(2)}) collective-permute-start(bf16[384,2048]{1,0:T(8,128)(2,1)} %get-tuple-element.29), channel_id=1, source_target_pairs={{0,4},{4,0},{8,12},{12,8},{16,20},{20,16},{24,28},{28,24},{1,5},{5... | collective-permute-start | bytes 4718600 | tf_op jit(solution)/shard_map/ppermute | solution.py:229
  5.9 13.5 %collective-permute-start.2 = (bf16[768,256]{1,0:T(8,128)(2,1)S(1)}, bf16[768,256]{1,0:T(8,128)(2,1)S(1)}, u32[]{:S(2)}, u32[]{:S(2)}) collective-permute-start(bf16[768,256]{1,0:T(8,128)(2,1)S(1)} %pad_maximum_fusion.k_ref.v_ref), channel_id=1, source_target_pairs={{0,8},{4,12},{8,16},{12,20},{16,24},{20,28},{1,9},{5,13},{9,17},{1... | collective-permute-start | bytes 1179656 | tf_op jit(solution)/shard_map/ppermute | solution.py:249
  19.4 12.1 %collective-permute-start.3 = (bf16[768,256]{1,0:T(8,128)(2,1)S(1)}, bf16[768,256]{1,0:T(8,128)(2,1)S(1)}, u32[]{:S(2)}, u32[]{:S(2)}) collective-permute-start(bf16[768,256]{1,0:T(8,128)(2,1)S(1)} %collective-permute-done.2.k_ref.v_ref.refs_0_.refs_1_), channel_id=1, source_target_pairs={{0,8},{4,12},{8,16},{12,20},{16,24},{20,28},{1,9},{5,13},{9,17},{1... | collective-permute-start | bytes 1179656 | tf_op jit(solution)/shard_map/ppermute | solution.py:249
  31.4 56.0 %collective-permute-start.4 = (bf16[768,256]{1,0:T(8,128)(2,1)S(1)}, bf16[768,256]{1,0:T(8,128)(2,1)S(1)}, u32[]{:S(2)}, u32[]{:S(2)}) collective-permute-start(bf16[768,256]{1,0:T(8,128)(2,1)S(1)} %collective-permute-done.3.k_ref.v_ref.refs_2_.refs_3_), channel_id=1, source_target_pairs={{0,8},{4,12},{8,16},{12,20},{16,24},{20,28},{1,9},{5,13},{9,17},{1... | collective-permute-start | bytes 1179656 | tf_op jit(solution)/shard_map/ppermute | solution.py:249
  38.9 23.3 %copy-start = (bf16[768,2048]{1,0:T(8,128)(2,1)}, bf16[768,2048]{1,0:T(8,128)(2,1)S(1)}, u32[]{:S(2)}) copy-start(bf16[768,2048]{1,0:T(8,128)(2,1)S(1)} %maximum_select_fusion.q_ref) | copy-start | bytes 9437188
  156.0 70.5 %collective-permute-start.5 = (bf16[1024,128]{1,0:T(8,128)(2,1)S(1)}, bf16[1024,128]{1,0:T(8,128)(2,1)S(1)}, u32[]{:S(2)}, u32[]{:S(2)}) collective-permute-start(bf16[1024,128]{1,0:T(8,128)(2,1)S(1)} %get-tuple-element.30), channel_id=1, source_target_pairs={{0,8},{4,12},{8,16},{12,20},{16,24},{20,28},{24,0},{28,4},{1,9},{5... | collective-permute-start | bytes 786440 | tf_op jit(solution)/shard_map/ppermute | solution.py:318
  178.3 57.0 %collective-permute-start.6 = (bf16[1024,128]{1,0:T(8,128)(2,1)S(1)}, bf16[1024,128]{1,0:T(8,128)(2,1)S(1)}, u32[]{:S(2)}, u32[]{:S(2)}) collective-permute-start(bf16[1024,128]{1,0:T(8,128)(2,1)S(1)} %get-tuple-element.32), channel_id=1, source_target_pairs={{0,16},{4,20},{8,24},{12,28},{16,0},{20,4},{24,8},{28,12},{1,17},{... | collective-permute-start | bytes 786440 | tf_op jit(solution)/shard_map/ppermute | solution.py:318
  219.8 15.5 %collective-permute-start.7 = (bf16[1024,128]{1,0:T(8,128)(2,1)S(1)}, bf16[1024,128]{1,0:T(8,128)(2,1)S(1)}, u32[]{:S(2)}, u32[]{:S(2)}) collective-permute-start(bf16[1024,128]{1,0:T(8,128)(2,1)S(1)} %get-tuple-element.31), channel_id=1, source_target_pairs={{0,24},{4,28},{8,0},{12,4},{16,8},{20,12},{24,16},{28,20},{1,25},{... | collective-permute-start | bytes 786440 | tf_op jit(solution)/shard_map/ppermute | solution.py:318
  235.7 18.4 %collective-permute-start.8 = (bf16[1024,128]{1,0:T(8,128)(2,1)S(1)}, bf16[1024,128]{1,0:T(8,128)(2,1)S(1)}, u32[]{:S(2)}, u32[]{:S(2)}) collective-permute-start(bf16[1024,128]{1,0:T(8,128)(2,1)S(1)} %get-tuple-element.25), channel_id=1, source_target_pairs={{0,8},{4,12},{8,16},{12,20},{16,24},{20,28},{24,0},{28,4},{1,9},{5... | collective-permute-start | bytes 786440 | tf_op jit(solution)/shard_map/ppermute | solution.py:322
  247.4 14.4 %collective-permute-start.9 = (bf16[1024,128]{1,0:T(8,128)(2,1)S(1)}, bf16[1024,128]{1,0:T(8,128)(2,1)S(1)}, u32[]{:S(2)}, u32[]{:S(2)}) collective-permute-start(bf16[1024,128]{1,0:T(8,128)(2,1)S(1)} %get-tuple-element.25), channel_id=1, source_target_pairs={{0,16},{4,20},{8,24},{12,28},{16,0},{20,4},{24,8},{28,12},{1,17},{... | collective-permute-start | bytes 786440 | tf_op jit(solution)/shard_map/ppermute | solution.py:322
  247.4 17.0 %collective-permute-start.10 = (bf16[1024,128]{1,0:T(8,128)(2,1)S(1)}, bf16[1024,128]{1,0:T(8,128)(2,1)S(1)}, u32[]{:S(2)}, u32[]{:S(2)}) collective-permute-start(bf16[1024,128]{1,0:T(8,128)(2,1)S(1)} %get-tuple-element.25), channel_id=1, source_target_pairs={{0,24},{4,28},{8,0},{12,4},{16,8},{20,12},{24,16},{28,20},{1,25},{... | collective-permute-start | bytes 786440 | tf_op jit(solution)/shard_map/ppermute | solution.py:322
  264.5 2.7 %collective-permute-start.11 = (bf16[16,2,128,128]{3,2,1,0:T(8,128)(2,1)S(1)}, bf16[16,2,128,128]{3,2,1,0:T(8,128)(2,1)S(1)}, u32[]{:S(2)}, u32[]{:S(2)}) collective-permute-start(bf16[16,2,128,128]{3,2,1,0:T(8,128)(2,1)S(1)} %bitcast.15), channel_id=1, source_target_pairs={{0,4},{4,0},{8,12},{12,8},{16,20},{20,16},{24,28},{28,24},{1,5},{5... | collective-permute-start | bytes 3145736 | tf_op jit(solution)/shard_map/ppermute | solution.py:327
